TPU v7x, 32 devices: a whole 2x2x4 slice. The times are simulated.
32 devices in a mesh: groups: 2 (over y), tm: 4 (over z), dp: 2 (over x), state: 2 (over core).
Axes of the slice: x: 2, y: 2, z: 4, core: 2. Of those that a mesh axis runs over, the one named last changes fastest.
Arguments:
- frames: bfloat16 [4, 1024, 256], P(('groups', 'dp'), ('tm', 'state')), parts along dimension 0, may hold values from -6 to 6
- first_layer_weight: bfloat16 [3, 256, 128], replicated, may hold values from -0.21875 to 0.21875
- second_layer_weight: bfloat16 [3, 128, 128], replicated, may hold values from -0.3125 to 0.3125
- readout: float32 [256, 256], replicated, may hold values from -0.375 to 0.375
- obs_gain: float32 [256, 128], replicated, may hold values from -1 to 1
- transition: float32 [256, 256], replicated, may hold values from -1 to 1
- smoother_gain: float32 [256, 256], replicated, may hold values from -1 to 1
- smooth_blend: float32 [256, 256], replicated, may hold values from -1 to 1
Outputs:
- smoothed: float32 [4, 1024, 256], P(('groups', 'dp'), ('tm', 'state')), parts along dimension 0
- grad_first: float32 [6, 256, 128], P('groups'), parts along dimension 0
- grad_second: float32 [6, 128, 128], P('groups'), parts along dimension 0
- grad_readout: float32 [512, 256], P('groups'), parts along dimension 0
- loss: float32 [2], P('groups'), parts along dimension 0
There are 2 independent parts, one for each index of `groups`. A program takes and returns all parts, laid end to end along the dimension named above; an argument that names none is the same for every part. Nothing has to cross between parts.
All inputs are finite; a program needn't handle non-finite values.
Results may differ from a plain program's by a relative error of at most 0.0028.
Values may be sent and summed in bfloat16 or wider, within the bound.
A program may use at most 128 MiB of HBM per device.

v0:
```python
import jax
import jax.numpy as jnp
from jax import lax
from jax.sharding import PartitionSpec as P

KERNEL_TAPS = 3
FIRST_SPACING = 8
SECOND_SPACING = 64


HIGHEST = lax.Precision.HIGHEST


def prefix_2(array, axis, combine, identity, reverse):
    devices, here = (lax.axis_size(axis), lax.axis_index(axis))
    everything = jax.tree.map(lambda part: lax.all_gather(part, axis), array)
    start = jax.tree.map(
        lambda part, zero: jnp.broadcast_to(jnp.asarray(zero, part.dtype), part.shape),
        array,
        identity,
    )

    def turn(k, before):
        at = devices - 1 - k if reverse else k
        reached = at > here if reverse else at < here
        new = combine(before, jax.tree.map(lambda part: part[at], everything))
        return jax.tree.map(lambda a, b: jnp.where(reached, a, b), new, before)

    return lax.fori_loop(0, devices, turn, start)


def padded_2(array, sides, width):
    for axis, dim in sides:
        devices, length = (lax.axis_size(axis), array.shape[dim])
        up = [(i, (i + 1) % devices) for i in range(devices - 1)]
        down = [(j, i) for i, j in up]
        last = lax.slice_in_dim(array, length - width, length, axis=dim)
        first = lax.slice_in_dim(array, 0, width, axis=dim)
        before = lax.ppermute(last, axis, up)
        after = lax.ppermute(first, axis, down)
        array = jnp.concatenate([before, array, after], axis=dim)
    return array


def spaced_taps(padded, weight, gap, frame_length):
    total = jnp.dot(padded[0:frame_length], weight[0], preferred_element_type=jnp.float32)
    for tap_index in range(1, KERNEL_TAPS):
        start_row = tap_index * gap
        total = total + jnp.dot(
            padded[start_row : start_row + frame_length],
            weight[tap_index],
            preferred_element_type=jnp.float32,
        )
    return total


def spaced_taps_backward(padded, weight, gap, frame_length):
    total = jnp.zeros((frame_length, weight.shape[1]), jnp.float32)
    for tap_index in range(KERNEL_TAPS):
        start_row = (KERNEL_TAPS - 1 - tap_index) * gap
        total = total + jnp.dot(
            padded[start_row : start_row + frame_length],
            weight[tap_index].T,
            preferred_element_type=jnp.float32,
        )
    return total


def weight_gradient_pair(padded, cotangent, gap, frame_length):
    return jnp.stack(
        [
            jnp.einsum(
                "ts,tc->sc",
                padded[tap_index * gap : tap_index * gap + frame_length],
                cotangent,
                preferred_element_type=jnp.float32,
            )
            for tap_index in range(KERNEL_TAPS)
        ]
    )


def power_table(matrix, frame_length):
    powers_of = [matrix]
    while 1 << len(powers_of) <= frame_length:
        powers_of.append(jnp.dot(powers_of[-1], powers_of[-1], precision=HIGHEST))
    return powers_of


def full_power(powers_of, frame_length):
    result = None
    for level in range(len(powers_of)):
        if frame_length >> level & 1:
            result = powers_of[level]
    return result


def prefix(drive_rows, powers_of):
    frame_length = drive_rows.shape[0]
    running = drive_rows
    level = 0
    while 1 << level < frame_length:
        stride = 1 << level
        carried_in = jnp.dot(running[: frame_length - stride], powers_of[level], precision=HIGHEST)
        running = running + jnp.concatenate(
            [jnp.zeros((stride, running.shape[1]), jnp.float32), carried_in]
        )
        level += 1
    return running


def propagate(entering, powers_of, frame_length):
    carried_rows = jnp.dot(entering, powers_of[0], precision=HIGHEST)[None]
    level = 0
    while carried_rows.shape[0] < frame_length:
        further = jnp.dot(carried_rows, powers_of[level], precision=HIGHEST)
        carried_rows = jnp.concatenate([carried_rows, further])
        level += 1
    return carried_rows


def carry_in(block_end, block_power, reverse):
    width = block_end.shape[0]

    def combine(earlier, later):
        return (
            jnp.dot(earlier[0], later[0], precision=HIGHEST),
            jnp.dot(earlier[1], later[0], precision=HIGHEST) + later[1],
        )

    identity = (jnp.eye(width, dtype=jnp.float32), jnp.zeros((width,), jnp.float32))
    _, entering = prefix_2((block_power, block_end), ("tm", "state"), combine, identity, reverse)
    return entering


def recurrence(drive_rows, powers_of, reverse):
    frame_length = drive_rows.shape[0]
    ordered = drive_rows[::-1] if reverse else drive_rows
    block_power = full_power(powers_of, frame_length)
    running = prefix(ordered, powers_of)
    entering = carry_in(running[-1], block_power, reverse)
    running = running + propagate(entering, powers_of, frame_length)
    return running[::-1] if reverse else running


def body(
    frames,
    first_layer_weight,
    second_layer_weight,
    readout,
    obs_gain,
    transition,
    smoother_gain,
    smooth_blend,
):
    signal = frames[0]
    frame_length = signal.shape[0]
    first_receptive_span = KERNEL_TAPS // 2 * FIRST_SPACING
    second_receptive_span = KERNEL_TAPS // 2 * SECOND_SPACING
    input_padded = padded_2(signal, ((("tm", "state"), 0),), first_receptive_span)
    preactivation = spaced_taps(input_padded, first_layer_weight, FIRST_SPACING, frame_length)
    hidden = jax.nn.gelu(preactivation).astype(jnp.bfloat16)
    middle_padded = padded_2(hidden, ((("tm", "state"), 0),), second_receptive_span)
    encoded_frames = spaced_taps(middle_padded, second_layer_weight, SECOND_SPACING, frame_length)
    drive_rows = jnp.dot(encoded_frames, obs_gain.T, precision=HIGHEST)
    powers_a = power_table(transition, frame_length)
    powers_g = power_table(smoother_gain, frame_length)
    powers_at = [entry_mat.T for entry_mat in powers_a]
    powers_gt = [entry_mat.T for entry_mat in powers_g]
    frames_total = frame_length * lax.axis_size("tm") * lax.axis_size("state")
    position = lax.axis_index(("tm", "state")) * frame_length + jnp.arange(frame_length)
    is_last = (position == frames_total - 1)[:, None]
    filtered = recurrence(drive_rows, powers_at, False)
    blended = jnp.where(is_last, filtered, jnp.dot(filtered, smooth_blend.T, precision=HIGHEST))
    smoothed = recurrence(blended, powers_gt, True)
    miss = jnp.dot(smoothed, readout.T, precision=HIGHEST) - signal.astype(jnp.float32)
    windows_total = frames.shape[0] * lax.axis_size("dp")
    scale = 1.0 / (windows_total * frames_total)
    d_miss = miss * scale
    grad_read = jnp.dot(d_miss.T, smoothed, precision=HIGHEST)
    adj_smooth = recurrence(jnp.dot(d_miss, readout, precision=HIGHEST), powers_g, False)
    d_filtered = jnp.where(
        is_last, adj_smooth, jnp.dot(adj_smooth, smooth_blend, precision=HIGHEST)
    )
    adj_filter = recurrence(d_filtered, powers_a, True)
    observed_gradient = jnp.dot(adj_filter, obs_gain, precision=HIGHEST).astype(jnp.bfloat16)
    backward_padded = padded_2(observed_gradient, ((("tm", "state"), 0),), second_receptive_span)
    hidden_gradient = spaced_taps_backward(
        backward_padded, second_layer_weight, SECOND_SPACING, frame_length
    )
    _, gelu_back = jax.vjp(jax.nn.gelu, preactivation)
    preactivation_gradient = gelu_back(hidden_gradient)[0].astype(jnp.bfloat16)
    second_layer_gradient = weight_gradient_pair(
        middle_padded, observed_gradient, SECOND_SPACING, frame_length
    )
    first_layer_gradient = weight_gradient_pair(
        input_padded, preactivation_gradient, FIRST_SPACING, frame_length
    )
    loss_part = 0.5 * jnp.sum(miss * miss) * scale / signal.shape[1]
    summed = lax.psum(
        (first_layer_gradient, second_layer_gradient, grad_read, loss_part), ("tm", "dp", "state")
    )
    return (smoothed[None], summed[0], summed[1], summed[2], summed[3].reshape(1))


def solution(mesh):
    return jax.shard_map(
        body,
        mesh=mesh,
        in_specs=(P(("groups", "dp"), ("tm", "state"), None), P(), P(), P(), P(), P(), P(), P()),
        out_specs=(
            P(("groups", "dp"), ("tm", "state"), None),
            P("groups", None, None),
            P("groups", None, None),
            P("groups", None),
            P("groups"),
        ),
        check_vma=False,
    )
```

profile of v0, /device:TPU:1, one launch (start us, length us, event | category | flops | bytes accessed | tf_op | source)
XLA Modules:
  0.0 309.5 jit_solution(7936272497854799922)
XLA Ops:
  16.7 2.0 collective-permute-start.1
  18.7 4.5 %collective-permute-start = (bf16[8,256]{1,0:T(8,128)(2,1)S(1)}, bf16[8,256]{1,0:T(8,128)(2,1)S(1)}, u32[]{:S(2)}, u32[]{:S(2)}) collective-permute-start(bf16[8,256]{1,0:T(8,128)(2,1)S(1)} %get-tuple-element.596), channel_id=1, source_target_pairs={{0,1},{1,4},{4,5},{5,8},{8,9},{9,12},{12,13},{2,3},{3,6},{6,7},{7,... | collective-permute-start | bytes 12296 | tf_op jit(solution)/shard_map/ppermute | solution.py:39
  26.5 1.7 multiply_convert_fusion
  28.2 1.9 collective-permute-start.3
  31.0 3.6 %collective-permute-start.2 = (bf16[64,128]{1,0:T(8,128)(2,1)S(1)}, bf16[64,128]{1,0:T(8,128)(2,1)S(1)}, u32[]{:S(2)}, u32[]{:S(2)}) collective-permute-start(bf16[64,128]{1,0:T(8,128)(2,1)S(1)} %get-tuple-element.600), channel_id=1, source_target_pairs={{0,1},{1,4},{4,5},{5,8},{8,9},{9,12},{12,13},{2,3},{3,6},{6,7},{7,... | collective-permute-start | bytes 49160 | tf_op jit(solution)/shard_map/ppermute | solution.py:39
  41.9 13.5 %all-gather.4 = f32[8,1,256]{2,1,0:T(1,128)S(1)} all-gather(f32[1,1,256]{2,1,0:T(1,128)S(1)} %slice_bitcast_fusion.5), channel_id=1, replica_groups=mesh['groups'=2,'tm'=4,'dp'=2,'state'=2] {'tm','state'}, dimensions={0}, use_global_device_ids=true | all-gather | bytes 9216 | tf_op jit(solution)/shard_map/all_gather | solution.py:16
  55.4 2.9 copy.20
  58.3 10.1 %while.60 = (s32[]{:T(128)}, f32[256]{0:T(256)S(1)}, s32[]{:T(128)}, f32[8,256,256]{2,1,0:T(8,128)}, f32[8,256]{1,0:T(8,128)S(1)}, /*index=5*/s32[]{:T(128)}, s32[]{:T(128)}) while((s32[]{:T(128)}, f32[256]{0:T(256)S(1)}, s32[]{:T(128)}, f32[8,256,256]{2,1,0:T(8,128)}, f32[8,256]{1,0:T(8,128)S(1)}, /*index=5*/s32[]{:T(128)}, ...), condition=%wide.region_1.2_spmd.clone, body=%wide.region_0.1_spmd.clone.sunk | while | flops 787460 | bytes 272498 | solution.py:29
  72.3 1.8 concatenate.228
  75.2 3.8 %concatenate.229 = f32[64,256]{1,0:T(8,128)} concatenate(f32[1,256]{1,0:T(1,128)} %copy-done.24, f32[1,256]{1,0:T(1,128)} %copy-done.26, f32[2,256]{1,0:T(2,128)} %copy-done.22, f32[4,256]{1,0:T(4,128)} %copy-done.17, f32[8,256]{1,0:T(8,128)} %copy-done.15, f32[16,256]{1,0:T(8,128)S(1)} %fusion.232, f32[32,256]{1,0:T(8,128)S(1)} %fusion.233), dimensions={0} | concatenate | bytes 131072 | tf_op jit(solution)/shard_map/concatenate | solution.py:117
  79.1 1.8 fusion.234
  80.9 5.3 %concatenate.230 = f32[128,256]{1,0:T(8,128)} concatenate(f32[1,256]{1,0:T(1,128)} %copy-done.24, f32[1,256]{1,0:T(1,128)} %copy-done.26, f32[2,256]{1,0:T(2,128)} %copy-done.22, f32[4,256]{1,0:T(4,128)} %copy-done.17, f32[8,256]{1,0:T(8,128)} %copy-done.15, f32[16,256]{1,0:T(8,128)S(1)} %fusion.232, f32[32,256]{1,0:T(8,128)S(1)} %fusion.233, f32[64,256]{1,0:T(8,128)} %fusion.234), dimensions={0} | concatenate | bytes 262144 | tf_op jit(solution)/shard_map/concatenate | solution.py:117
  86.2 2.2 convolution_select_fusion.1
  98.5 8.7 %all-gather.5 = f32[8,1,256]{2,1,0:T(1,128)S(1)} all-gather(f32[1,1,256]{2,1,0:T(1,128)S(1)} %slice_bitcast_fusion.4), channel_id=1, replica_groups=mesh['groups'=2,'tm'=4,'dp'=2,'state'=2] {'tm','state'}, dimensions={0}, use_global_device_ids=true | all-gather | bytes 9216 | tf_op jit(solution)/shard_map/all_gather | solution.py:16
  107.2 3.0 copy.21
  110.2 10.2 %while.61 = (s32[]{:T(128)}, f32[256]{0:T(256)S(1)}, s32[]{:T(128)}, f32[8,256,256]{2,1,0:T(8,128)}, f32[8,256]{1,0:T(8,128)S(1)}, /*index=5*/s32[]{:T(128)}, s32[]{:T(128)}, s32[]{:T(128)}, s32[]{:T(128)}) while((s32[]{:T(128)}, f32[256]{0:T(256)S(1)}, s32[]{:T(128)}, f32[8,256,256]{2,1,0:T(8,128)}, f32[8,256]{1,0:T(8,128)S(1)}, ...), condition=%wide.region_3.4_spmd.clone, body=%wide.region_2.3_spmd.clone.sunk | while | flops 787464 | bytes 272560 | solution.py:29
  124.6 1.8 concatenate.242
  127.5 3.8 %concatenate.243 = f32[64,256]{1,0:T(8,128)} concatenate(f32[1,256]{1,0:T(1,128)} %copy-done.25, f32[1,256]{1,0:T(1,128)} %copy-done.27, f32[2,256]{1,0:T(2,128)} %copy-done.23, f32[4,256]{1,0:T(4,128)} %copy-done.18, f32[8,256]{1,0:T(8,128)} %copy-done.16, f32[16,256]{1,0:T(8,128)S(1)} %fusion.243, f32[32,256]{1,0:T(8,128)S(1)} %fusion.244), dimensions={0} | concatenate | bytes 131072 | tf_op jit(solution)/shard_map/concatenate | solution.py:117
  131.3 1.8 fusion.245
  133.1 5.3 %concatenate.244 = f32[128,256]{1,0:T(8,128)} concatenate(f32[1,256]{1,0:T(1,128)} %copy-done.25, f32[1,256]{1,0:T(1,128)} %copy-done.27, f32[2,256]{1,0:T(2,128)} %copy-done.23, f32[4,256]{1,0:T(4,128)} %copy-done.18, f32[8,256]{1,0:T(8,128)} %copy-done.16, f32[16,256]{1,0:T(8,128)S(1)} %fusion.243, f32[32,256]{1,0:T(8,128)S(1)} %fusion.244, f32[64,256]{1,0:T(8,128)} %fusion.245), dimensions={0} | concatenate | bytes 262144 | tf_op jit(solution)/shard_map/concatenate | solution.py:117
  141.6 2.0 multiply_reduce_fusion
  147.7 10.3 %all-gather.6 = f32[8,1,256]{2,1,0:T(1,128)S(1)} all-gather(f32[1,1,256]{2,1,0:T(1,128)S(1)} %slice_bitcast_fusion.3), channel_id=1, replica_groups=mesh['groups'=2,'tm'=4,'dp'=2,'state'=2] {'tm','state'}, dimensions={0}, use_global_device_ids=true | all-gather | bytes 9216 | tf_op jit(solution)/shard_map/all_gather | solution.py:16
  158.1 10.1 %while.62 = (s32[]{:T(128)}, f32[256]{0:T(256)S(1)}, s32[]{:T(128)}, f32[8,256,256]{2,1,0:T(8,128)}, f32[8,256]{1,0:T(8,128)S(1)}, /*index=5*/s32[]{:T(128)}, s32[]{:T(128)}) while((s32[]{:T(128)}, f32[256]{0:T(256)S(1)}, s32[]{:T(128)}, f32[8,256,256]{2,1,0:T(8,128)}, f32[8,256]{1,0:T(8,128)S(1)}, /*index=5*/s32[]{:T(128)}, ...), condition=%wide.region_5.6_spmd.clone, body=%wide.region_4.5_spmd.clone.sunk | while | flops 787460 | bytes 272498 | solution.py:29
  174.8 8.7 %all-gather.7 = f32[8,1,256]{2,1,0:T(1,128)S(1)} all-gather(f32[1,1,256]{2,1,0:T(1,128)S(1)} %slice_bitcast_fusion.2), channel_id=1, replica_groups=mesh['groups'=2,'tm'=4,'dp'=2,'state'=2] {'tm','state'}, dimensions={0}, use_global_device_ids=true | all-gather | bytes 9216 | tf_op jit(solution)/shard_map/all_gather | solution.py:16
  183.5 10.1 %while.63 = (s32[]{:T(128)}, f32[256]{0:T(256)S(1)}, s32[]{:T(128)}, f32[8,256,256]{2,1,0:T(8,128)}, f32[8,256]{1,0:T(8,128)S(1)}, /*index=5*/s32[]{:T(128)}, s32[]{:T(128)}, s32[]{:T(128)}, s32[]{:T(128)}) while((s32[]{:T(128)}, f32[256]{0:T(256)S(1)}, s32[]{:T(128)}, f32[8,256,256]{2,1,0:T(8,128)}, f32[8,256]{1,0:T(8,128)S(1)}, ...), condition=%wide.region_7.8_spmd.clone, body=%wide.region_6.7_spmd.clone.sunk | while | flops 787464 | bytes 272560 | solution.py:29
  197.6 3.4 %collective-permute-start.5 = (bf16[64,128]{1,0:T(8,128)(2,1)S(1)}, bf16[64,128]{1,0:T(8,128)(2,1)S(1)}, u32[]{:S(2)}, u32[]{:S(2)}) collective-permute-start(bf16[64,128]{1,0:T(8,128)(2,1)S(1)} %get-tuple-element.599), channel_id=1, source_target_pairs={{0,1},{1,4},{4,5},{5,8},{8,9},{9,12},{12,13},{2,3},{3,6},{6,7},{7,... | collective-permute-start | bytes 49160 | tf_op jit(solution)/shard_map/ppermute | solution.py:39
  201.0 1.9 collective-permute-start.4
  204.1 1.9 collective-permute-done.4
  208.3 28.3 %psum.31 = f32[1]{0:T(128)} all-reduce(f32[1]{0:T(128)} %bitcast.45), channel_id=1, replica_groups=mesh['groups'=2,'tm'=4,'dp'=2,'state'=2] {'tm','dp','state'}, use_global_device_ids=true, to_apply=%region_12.13 | all-reduce | flops 1 | bytes 8 | tf_op jit(solution)/shard_map/psum | solution.py:200
  236.6 61.3 %all-reduce.31.cloned.1.call-done = (f32[3,256,128]{2,1,0:T(8,128)}, f32[3,128,128]{2,1,0:T(8,128)}, f32[256,256]{1,0:T(8,128)}) async-done(((f32[3,256,128]{2,1,0:T(8,128)}, f32[3,128,128]{2,1,0:T(8,128)}, f32[256,256]{1,0:T(8,128)}), (f32[3,256,128]{2,1,0:T(8,128)}, f32[3,128,128]{2,1,0:T(8,128)}, f32[256,256]{1,0:T(8,128)})) %all-reduce.31.cloned.1.call-update) | async-done | bytes 851984 | tf_op jit(solution)/shard_map/psum | solution.py:200
  297.9 1.8 copy.61
  301.3 1.7 copy.63
  (381 shorter events, 101.6 us)
Async XLA Ops:
  7.2 4.6 %copy-start = (f32[256,256]{1,0:T(8,128)S(1)}, f32[256,256]{1,0:T(8,128)}, u32[]{:S(2)}) copy-start(f32[256,256]{1,0:T(8,128)} %param.22) | copy-start | bytes 786436
  7.2 48.2 %all-gather.13.cloned.1.call-start = ((), (), s32[]{:S(2)}) async-start(), calls=%async_computation | async-start | bytes 2359296 | tf_op jit(solution)/shard_map/all_gather | solution.py:16
  11.7 95.5 %all-gather.15.cloned.1.call-start = ((), (), s32[]{:S(2)}) async-start(), calls=%async_computation.1 | async-start | bytes 2359296 | tf_op jit(solution)/shard_map/all_gather | solution.py:16
  12.5 4.2 %copy-start.5 = (bf16[1,128,256]{2,1,0:T(8,128)(2,1)S(1)}, bf16[1,128,256]{2,1,0:T(8,128)(2,1)}, u32[]{:S(2)}) copy-start(bf16[1,128,256]{2,1,0:T(8,128)(2,1)} %param.16) | copy-start | bytes 196612
  14.4 23.9 %copy-start.1 = (f32[256,256]{1,0:T(8,128)S(1)}, f32[256,256]{1,0:T(8,128)}, u32[]{:S(2)}) copy-start(f32[256,256]{1,0:T(8,128)} %param.21) | copy-start | bytes 786436
  15.9 142.1 %all-gather.17.cloned.1.call-start = ((), (), s32[]{:S(2)}) async-start(), calls=%async_computation.2 | async-start | bytes 2359296 | tf_op jit(solution)/shard_map/all_gather | solution.py:16
  16.7 166.8 %all-gather.19.cloned.1.call-start = ((), (), s32[]{:S(2)}) async-start(), calls=%async_computation.3 | async-start | bytes 2359296 | tf_op jit(solution)/shard_map/all_gather | solution.py:16
  16.7 8.8 %collective-permute-start.1 = (bf16[8,256]{1,0:T(8,128)(2,1)S(1)}, bf16[8,256]{1,0:T(8,128)(2,1)S(1)}, u32[]{:S(2)}, u32[]{:S(2)}) collective-permute-start(bf16[8,256]{1,0:T(8,128)(2,1)S(1)} %get-tuple-element.597), channel_id=1, source_target_pairs={{1,0},{4,1},{5,4},{8,5},{9,8},{12,9},{13,12},{3,2},{6,3},{7,6},{10... | collective-permute-start | bytes 12296 | tf_op jit(solution)/shard_map/ppermute | solution.py:40
  18.7 7.8 %collective-permute-start = (bf16[8,256]{1,0:T(8,128)(2,1)S(1)}, bf16[8,256]{1,0:T(8,128)(2,1)S(1)}, u32[]{:S(2)}, u32[]{:S(2)}) collective-permute-start(bf16[8,256]{1,0:T(8,128)(2,1)S(1)} %get-tuple-element.596), channel_id=1, source_target_pairs={{0,1},{1,4},{4,5},{5,8},{8,9},{9,12},{12,13},{2,3},{3,6},{6,7},{7,... | collective-permute-start | bytes 12296 | tf_op jit(solution)/shard_map/ppermute | solution.py:39
  23.3 274.7 %all-reduce.31.cloned.1.call-start = ((), (), s32[]{:S(2)}) async-start(), calls=%async_computation.4 | async-start | bytes 1703936 | tf_op jit(solution)/shard_map/psum | solution.py:200
  26.5 13.5 %copy-start.34 = (bf16[8,256]{1,0:T(8,128)(2,1)}, bf16[8,256]{1,0:T(8,128)(2,1)S(1)}, u32[]{:S(2)}) copy-start(bf16[8,256]{1,0:T(8,128)(2,1)S(1)} %collective-permute-done) | copy-start | bytes 12292
  28.2 6.5 %collective-permute-start.3 = (bf16[64,128]{1,0:T(8,128)(2,1)S(1)}, bf16[64,128]{1,0:T(8,128)(2,1)S(1)}, u32[]{:S(2)}, u32[]{:S(2)}) collective-permute-start(bf16[64,128]{1,0:T(8,128)(2,1)S(1)} %get-tuple-element.601), channel_id=1, source_target_pairs={{1,0},{4,1},{5,4},{8,5},{9,8},{12,9},{13,12},{3,2},{6,3},{7,6},{10... | collective-permute-start | bytes 49160 | tf_op jit(solution)/shard_map/ppermute | solution.py:40
  31.0 4.6 %collective-permute-start.2 = (bf16[64,128]{1,0:T(8,128)(2,1)S(1)}, bf16[64,128]{1,0:T(8,128)(2,1)S(1)}, u32[]{:S(2)}, u32[]{:S(2)}) collective-permute-start(bf16[64,128]{1,0:T(8,128)(2,1)S(1)} %get-tuple-element.600), channel_id=1, source_target_pairs={{0,1},{1,4},{4,5},{5,8},{8,9},{9,12},{12,13},{2,3},{3,6},{6,7},{7,... | collective-permute-start | bytes 49160 | tf_op jit(solution)/shard_map/ppermute | solution.py:39
  68.7 3.6 %copy-start.24 = (f32[1,256]{1,0:T(1,128)}, f32[1,256]{1,0:T(1,128)S(1)}, u32[]{:S(2)}) copy-start(f32[1,256]{1,0:T(1,128)S(1)} %fusion.21) | copy-start | bytes 3076
  69.0 3.3 %copy-start.26 = (f32[1,256]{1,0:T(1,128)}, f32[1,256]{1,0:T(1,128)S(1)}, u32[]{:S(2)}) copy-start(f32[1,256]{1,0:T(1,128)S(1)} %fusion.194) | copy-start | bytes 3076
  69.3 3.0 copy-start.22
  93.1 3.6 %copy-start.3 = (f32[256,256]{1,0:T(8,128)S(1)}, f32[256,256]{1,0:T(8,128)}, u32[]{:S(2)}) copy-start(f32[256,256]{1,0:T(8,128)} %copy-done.2) | copy-start | bytes 786436
  107.2 3.0 copy-start.21
  120.7 3.9 %copy-start.25 = (f32[1,256]{1,0:T(1,128)}, f32[1,256]{1,0:T(1,128)S(1)}, u32[]{:S(2)}) copy-start(f32[1,256]{1,0:T(1,128)S(1)} %fusion.19) | copy-start | bytes 3076
  121.0 3.6 %copy-start.27 = (f32[1,256]{1,0:T(1,128)}, f32[1,256]{1,0:T(1,128)S(1)}, u32[]{:S(2)}) copy-start(f32[1,256]{1,0:T(1,128)S(1)} %fusion.192) | copy-start | bytes 3076
  121.3 3.2 %copy-start.23 = (f32[2,256]{1,0:T(2,128)}, f32[2,256]{1,0:T(2,128)S(1)}, u32[]{:S(2)}) copy-start(f32[2,256]{1,0:T(2,128)S(1)} %fusion.176) | copy-start | bytes 6148
  121.6 2.9 copy-start.18
  145.6 12.5 %copy-start.20 = (f32[256]{0:T(256)S(1)}, f32[256]{0:T(256)}, u32[]{:S(2)}) copy-start(f32[256]{0:T(256)} %custom-call.2) | copy-start | bytes 3076
  158.1 13.0 %copy-start.36 = (pred[128]{0:T(512)(128)(4,1)S(1)}, pred[128]{0:T(512)(128)(4,1)}, u32[]{:S(2)}) copy-start(pred[128]{0:T(512)(128)(4,1)} %add_compare_fusion) | copy-start | bytes 388
  173.2 10.2 %copy-start.19 = (f32[256]{0:T(256)S(1)}, f32[256]{0:T(256)}, u32[]{:S(2)}) copy-start(f32[256]{0:T(256)} %custom-call.3) | copy-start | bytes 3076
  194.1 8.8 %copy-start.29 = (bf16[64,128]{1,0:T(8,128)(2,1)S(1)}, bf16[64,128]{1,0:T(8,128)(2,1)}, u32[]{:S(2)}) copy-start(bf16[64,128]{1,0:T(8,128)(2,1)} %copy-done.28) | copy-start | bytes 49156
  194.1 9.0 %copy-start.31 = (bf16[64,128]{1,0:T(8,128)(2,1)S(1)}, bf16[64,128]{1,0:T(8,128)(2,1)}, u32[]{:S(2)}) copy-start(bf16[64,128]{1,0:T(8,128)(2,1)} %copy-done.30) | copy-start | bytes 49156
  194.8 11.2 %copy-start.37 = (f32[128,128]{1,0:T(8,128)S(1)}, f32[128,128]{1,0:T(8,128)}, u32[]{:S(2)}) copy-start(f32[128,128]{1,0:T(8,128)} %get-tuple-element.603) | copy-start | bytes 196612
  195.4 11.1 %copy-start.33 = (bf16[8,256]{1,0:T(8,128)(2,1)S(1)}, bf16[8,256]{1,0:T(8,128)(2,1)}, u32[]{:S(2)}) copy-start(bf16[8,256]{1,0:T(8,128)(2,1)} %copy-done.32) | copy-start | bytes 12292
  195.4 11.2 %copy-start.35 = (bf16[8,256]{1,0:T(8,128)(2,1)S(1)}, bf16[8,256]{1,0:T(8,128)(2,1)}, u32[]{:S(2)}) copy-start(bf16[8,256]{1,0:T(8,128)(2,1)} %copy-done.34) | copy-start | bytes 12292
  197.6 6.4 %collective-permute-start.5 = (bf16[64,128]{1,0:T(8,128)(2,1)S(1)}, bf16[64,128]{1,0:T(8,128)(2,1)S(1)}, u32[]{:S(2)}, u32[]{:S(2)}) collective-permute-start(bf16[64,128]{1,0:T(8,128)(2,1)S(1)} %get-tuple-element.599), channel_id=1, source_target_pairs={{0,1},{1,4},{4,5},{5,8},{8,9},{9,12},{12,13},{2,3},{3,6},{6,7},{7,... | collective-permute-start | bytes 49160 | tf_op jit(solution)/shard_map/ppermute | solution.py:39
  201.0 5.1 %collective-permute-start.4 = (bf16[64,128]{1,0:T(8,128)(2,1)S(1)}, bf16[64,128]{1,0:T(8,128)(2,1)S(1)}, u32[]{:S(2)}, u32[]{:S(2)}) collective-permute-start(bf16[64,128]{1,0:T(8,128)(2,1)S(1)} %get-tuple-element.598), channel_id=1, source_target_pairs={{1,0},{4,1},{5,4},{8,5},{9,8},{12,9},{13,12},{3,2},{6,3},{7,6},{10... | collective-permute-start | bytes 49160 | tf_op jit(solution)/shard_map/ppermute | solution.py:40
  (17 other events, 29.2 us)
Sparse Core Ops, SparseCore 0:
  11.8 31.7 all-gather.12
  45.2 28.6 all-gather.14
  75.5 28.6 all-gather.16
  106.2 28.6 all-gather.18
  207.8 90.1 all-reduce.30
where the time goes:
time: 313 us; the launch traced here: 310 us
  matrix products  88.9 us (28%)
  blocking collectives  69.6 us (22%)
  waiting for transfers between devices  64.1 us (20%)
  local copies, waits for them, and re-layouts  46.8 us (15%)
  starting transfers between devices  17.6 us (6%)
  between operations  15.7 us (5%)
  other arithmetic  5.64 us (2%)
    psum x1, waiting for transfers between devices, body(): lax.psum((first_layer_gradient, second_layer_gradient, grad_read, loss_pa...  61.3 us
    all_gather x4, blocking collectives, prefix_2(): everything = jax.tree.map(lambda part: lax.all_gather(part, axis), array)  41.2 us
    dot_general x32, matrix products, combine(): jnp.dot(earlier[1], later[0], precision=HIGHEST) + later[1]  37.3 us
    psum x1, blocking collectives, body(): lax.psum((first_layer_gradient, second_layer_gradient, grad_read, loss_pa...  28.3 us
    concatenate x16, local copies, waits for them, and re-layouts, propagate(): carried_rows = jnp.concatenate([carried_rows, further])  24.7 us
    dot_general x28, matrix products, propagate(): further = jnp.dot(carried_rows, powers_of[level], precision=HIGHEST)  14.8 us
    unnamed x89, local copies, waits for them, and re-layouts  14.5 us
    ppermute x3, starting transfers between devices, padded_2(): before = lax.ppermute(last, axis, up)  11.6 us
  transfers between devices with their start and end apart: 11, of which 3 were waited for; matrix products, arithmetic and copies ran while one was open for 37% of the time, Pallas kernels for 0%

commit v1 on v0

v1 whole, which is shorter than its diff:
```python
import functools
import math

import jax
import jax.numpy as jnp
from jax import lax
from jax.experimental import pallas as pl
from jax.experimental.pallas import tpu as pltpu
from jax.sharding import PartitionSpec as P

KERNEL_TAPS = 3
FIRST_SPACING = 8
SECOND_SPACING = 64
EDGE = 80
AXES = ("state", "dp", "tm")
SHORT, WIDE = (jnp.bfloat16, jnp.float32)


def split(array):
    high = array.astype(SHORT)
    return high, (array - high.astype(WIDE)).astype(SHORT)


def dot(a, b, contract):
    return lax.dot_general(a, b, (contract, ((), ())), preferred_element_type=WIDE)


def product(a, b, turned=False):
    contract = ((1,), (1 if turned else 0,))
    return dot(a[0], b[0], contract) + (dot(a[0], b[1], contract) + dot(a[1], b[0], contract))


def square(matrix):
    high = matrix.astype(SHORT)
    left = matrix - high.astype(WIDE)
    middle = left.astype(SHORT)
    low = (left - middle.astype(WIDE)).astype(SHORT)
    contract = ((1,), (0,))
    small = dot(high, low, contract) + dot(low, high, contract) + dot(middle, middle, contract)
    cross = dot(high, middle, contract) + dot(middle, high, contract)
    return dot(high, high, contract) + (cross + small)


def inner(a, b):
    contract = ((0,), (0,))
    return dot(a[0], b[0], contract) + (dot(a[0], b[1], contract) + dot(a[1], b[0], contract))


def remote(src, dst, send_sem, recv_sem, device):
    return pltpu.make_async_remote_copy(
        src_ref=src,
        dst_ref=dst,
        send_sem=send_sem,
        recv_sem=recv_sem,
        device_id=device,
        device_id_type=pl.DeviceIdType.MESH,
    )


class Reduction:
    def __init__(self, rows, sizes, refs):
        (self.total, self.full), self.sends, self.slots = refs[:2], refs[2:5], refs[5:8]
        self.held, (self.send_sem, self.recv_sem) = refs[8:10], refs[10:12]
        self.held = (self.total,) + tuple(self.held)
        self.sizes, self.pending = sizes, []
        self.at = [lax.axis_index(axis) for axis in AXES]
        self.piece = []
        for size in sizes:
            rows //= size
            self.piece.append(rows)

    def region(self, level, index):
        offset = index * self.piece[level]
        for above in range(level):
            offset = offset + self.at[above] * self.piece[above]
        return pl.ds(pl.multiple_of(offset, 16), self.piece[level])

    def start_scatter(self, level):
        self.sends[level][...] = self.held[level][...].astype(SHORT)
        for step in range(1, self.sizes[level]):
            to = lax.rem(self.at[level] + step, self.sizes[level])
            start = pl.multiple_of(to * self.piece[level], 16)
            copy = remote(
                self.sends[level].at[pl.ds(start, self.piece[level])],
                self.slots[level].at[step - 1],
                self.send_sem.at[level, step - 1],
                self.recv_sem.at[level, step - 1],
                {AXES[level]: to},
            )
            copy.start()
            self.pending.append(copy)

    def finish_scatter(self, level):
        for copy in self.pending[-(self.sizes[level] - 1) :]:
            copy.wait_recv()
        start = pl.multiple_of(self.at[level] * self.piece[level], 16)
        value = self.held[level][pl.ds(start, self.piece[level])]
        for step in range(1, self.sizes[level]):
            value = value + self.slots[level][step - 1].astype(WIDE)
        if level + 1 < len(AXES):
            self.held[level + 1][...] = value
        else:
            self.full[self.region(level, self.at[level])] = value.astype(self.full.dtype)

    def start_gather(self, level):
        mine = self.full.at[self.region(level, self.at[level])]
        for step in range(1, self.sizes[level]):
            to = lax.rem(self.at[level] + step, self.sizes[level])
            copy = remote(
                mine,
                mine,
                self.send_sem.at[3 + level, step - 1],
                self.recv_sem.at[3 + level, step - 1],
                {AXES[level]: to},
            )
            copy.start()
            self.pending.append(copy)

    def finish_gather(self, level):
        for step in range(1, self.sizes[level]):
            size = self.sizes[level]
            source = lax.rem(self.at[level] + size - step, size)
            theirs = self.full.at[self.region(level, source)]
            remote(
                theirs,
                theirs,
                self.send_sem.at[3 + level, step - 1],
                self.recv_sem.at[3 + level, step - 1],
                {AXES[level]: source},
            ).wait_recv()

    def drain(self):
        for copy in self.pending:
            copy.wait_send()


def kernel(dims, *refs):
    blocks, cores, sizes, windows, frames_total, levels = dims
    (frames_ref, first_ref, second_ref, readout_ref, gain_ref) = refs[:5]
    (transition_ref, smoother_ref, blend_ref) = refs[5:8]
    (smoothed_out, first_out, second_out, read_out, loss_out) = refs[8:13]
    (ext, power_high, power_low, ends, arrivals, slope) = refs[13:19]
    (halo_send, halo_recv, carry_send, carry_recv) = refs[19:23]
    (loss_send, loss_slots, loss_send_sem, loss_recv_sem) = refs[23:27]
    refs_a, refs_b = refs[27:39], refs[39:51]
    frame_length = frames_ref.shape[1]
    state = transition_ref.shape[0]
    local_levels = frame_length.bit_length() - 1
    place = lax.axis_index("tm") * cores + lax.axis_index("state")
    first_block, last_block = place == 0, place == blocks - 1

    def device(at):
        return {"tm": at // cores, "state": lax.rem(at, cores)}

    ext[...] = jnp.zeros_like(ext)
    arrivals[...] = jnp.zeros_like(arrivals)
    ext[EDGE : EDGE + frame_length] = frames_ref[0]
    barrier = pltpu.get_barrier_semaphore()
    for step in range(1, blocks):
        pl.semaphore_signal(
            barrier,
            inc=1,
            device_id=device(lax.rem(place + step, blocks)),
            device_id_type=pl.DeviceIdType.MESH,
        )
    for step in range(1, sizes[1]):
        pl.semaphore_signal(
            barrier,
            inc=1,
            device_id={"dp": lax.rem(lax.axis_index("dp") + step, sizes[1])},
            device_id_type=pl.DeviceIdType.MESH,
        )
    pl.semaphore_wait(barrier, blocks - 1 + sizes[1] - 1)

    def to_next():
        return remote(
            frames_ref.at[0, frame_length - EDGE : frame_length],
            ext.at[0:EDGE],
            halo_send.at[0],
            halo_recv.at[0],
            device(lax.rem(place + 1, blocks)),
        )

    def to_previous():
        return remote(
            frames_ref.at[0, 0:EDGE],
            ext.at[EDGE + frame_length : 2 * EDGE + frame_length],
            halo_send.at[1],
            halo_recv.at[1],
            device(lax.rem(place + blocks - 1, blocks)),
        )

    @pl.when(jnp.logical_not(last_block))
    def _():
        to_next().start()

    @pl.when(jnp.logical_not(first_block))
    def _():
        to_previous().start()

    def power(which, level):
        return power_high[which, level], power_low[which, level]

    for which, ref in enumerate((transition_ref, smoother_ref)):
        held = ref[...]
        for level in range(levels):
            power_high[which, level], power_low[which, level] = split(held)
            if level + 1 < levels:
                held = square(held)

    gain, readout, blend = [split(ref[...]) for ref in (gain_ref, readout_ref, blend_ref)]

    @pl.when(jnp.logical_not(first_block))
    def _():
        to_next().wait_recv()

    @pl.when(jnp.logical_not(last_block))
    def _():
        to_previous().wait_recv()

    reach = frame_length + 2 * SECOND_SPACING
    low = EDGE - SECOND_SPACING
    taps = jnp.concatenate([first_ref[tap] for tap in range(KERNEL_TAPS)], axis=1)
    partial = dot(ext[...], taps, ((1,), (0,)))
    channels = second_ref.shape[2]
    preact = sum(
        partial[
            low + (tap - 1) * FIRST_SPACING : low + (tap - 1) * FIRST_SPACING + reach,
            tap * channels : (tap + 1) * channels,
        ]
        for tap in range(KERNEL_TAPS)
    )
    where_row = lax.broadcasted_iota(jnp.int32, (reach, channels), 0)
    begin = jnp.where(first_block, SECOND_SPACING, 0)
    end = jnp.where(last_block, SECOND_SPACING + frame_length, reach)
    inside = jnp.logical_and(where_row >= begin, where_row < end)
    root = math.sqrt(2.0 / math.pi)
    squared = preact * preact
    bent = jnp.tanh(root * (preact + 0.044715 * (squared * preact)))
    half = 0.5 * (1.0 + bent)
    hidden = jnp.where(inside, preact * half, 0.0).astype(SHORT)
    bend = 0.5 * preact * (1.0 - bent * bent) * (root * (1.0 + 3 * 0.044715 * squared))
    slope[...] = jnp.where(inside, half + bend, 0.0)
    spaced = jnp.concatenate(
        [
            hidden[tap * SECOND_SPACING : tap * SECOND_SPACING + frame_length]
            for tap in range(KERNEL_TAPS)
        ],
        axis=1,
    )
    second = jnp.concatenate([second_ref[tap] for tap in range(KERNEL_TAPS)], axis=0)
    observed = dot(spaced, second, ((1,), (0,)))
    drive = product(split(observed), gain, True)

    row = lax.broadcasted_iota(jnp.int32, (frame_length, state), 0)
    row8 = lax.broadcasted_iota(jnp.int32, (8, state), 0)

    def local_scan(running, which, turned, reverse):
        for level in range(local_levels):
            stride = 1 << level
            matrix = power(which, level)
            if stride < 8:
                moved = pltpu.roll(running, frame_length - stride if reverse else stride, 0)
                kept = row < frame_length - stride if reverse else row >= stride
                moved = jnp.where(kept, moved, 0.0)
                running = running + product(split(moved), matrix, turned)
            elif reverse:
                added = product(split(running[stride:]), matrix, turned)
                running = jnp.concatenate(
                    [running[: frame_length - stride] + added, running[frame_length - stride :]]
                )
            else:
                added = product(split(running[: frame_length - stride]), matrix, turned)
                running = jnp.concatenate([running[:stride], running[stride:] + added])
        return running

    def carry_copy(index, step, reverse):
        to = lax.rem(place + (blocks - step if reverse else step), blocks)
        return remote(
            ends.at[index],
            arrivals.at[index, step - 1],
            carry_send.at[index, step - 1],
            carry_recv.at[index, step - 1],
            device(to),
        )

    def has_later(step, reverse):
        return place >= step if reverse else place + step < blocks

    def start_carry(index, running, reverse):
        ends[index] = running[0:1] if reverse else running[frame_length - 1 :]
        for step in range(1, blocks):

            @pl.when(has_later(step, reverse))
            def _():
                carry_copy(index, step, reverse).start()

    def finish_carry(index, which, turned, reverse):
        for step in range(1, blocks):

            @pl.when(has_later(step, not reverse))
            def _():
                carry_copy(index, step, reverse).wait_recv()

        slots = arrivals.shape[1]
        entering = arrivals[index].reshape(slots, state)
        level = 0
        while 1 << level < blocks:
            nearer = pltpu.roll(entering, slots - (1 << level), 0)
            matrix = power(which, local_levels + level)
            entering = entering + product(split(nearer), matrix, turned)
            level += 1
        rows = jnp.broadcast_to(entering[0:1], (8, state))
        rows = product(split(rows), power(which, 0), turned)
        exponent = 7 - row8 if reverse else row8
        for level in range(local_levels):
            further = product(split(rows), power(which, level), turned)
            if level < 3:
                rows = jnp.where((exponent >> level) % 2 == 1, further, rows)
            else:
                rows = jnp.concatenate([further, rows] if reverse else [rows, further])
        return rows

    def drain_carry(index, reverse):
        for step in range(1, blocks):

            @pl.when(has_later(step, reverse))
            def _():
                carry_copy(index, step, reverse).wait_send()

    ending = jnp.logical_and(last_block, row == frame_length - 1)

    filtered = local_scan(drive, 0, True, False)
    start_carry(0, filtered, False)
    filtered = filtered + finish_carry(0, 0, True, False)
    blended = jnp.where(ending, filtered, product(split(filtered), blend, True))
    smoothed = local_scan(blended, 1, True, True)
    start_carry(1, smoothed, True)
    smoothed = smoothed + finish_carry(1, 1, True, True)
    smoothed_out[0] = smoothed

    smoothed_pair = split(smoothed)
    miss = product(smoothed_pair, readout, True) - frames_ref[0].astype(WIDE)
    scale = 1.0 / (windows * frames_total)
    miss_pair = split(miss * scale)
    adj_smooth = local_scan(product(miss_pair, readout), 1, False, False)
    start_carry(2, adj_smooth, False)

    reduce_a = Reduction(refs_a[0].shape[0], sizes, refs_a)
    reduce_b = Reduction(refs_b[0].shape[0], sizes, refs_b)
    grad_read = inner(miss_pair, smoothed_pair)
    read_rows = 2 * state
    if refs_a[0].shape[0] > read_rows:
        refs_a[0][read_rows:] = jnp.zeros((refs_a[0].shape[0] - read_rows, 128), WIDE)
    refs_a[0][0:state] = grad_read[:, 0:128]
    refs_a[0][state:read_rows] = grad_read[:, 128:256]
    reduce_a.start_scatter(0)
    loss = jnp.sum(miss * miss, axis=0, keepdims=True)
    loss = (loss[:, 0:128] + loss[:, 128:256]) * (0.5 * scale / state)

    loss_pending = []

    def start_loss(level, value):
        loss_send[level] = value
        here = lax.axis_index(AXES[level])
        for step in range(1, sizes[level]):
            to = lax.rem(here + step, sizes[level])
            copy = remote(
                loss_send.at[level],
                loss_slots.at[level, here],
                loss_send_sem.at[level, step - 1],
                loss_recv_sem.at[level, step - 1],
                {AXES[level]: to},
            )
            copy.start()
            loss_pending.append(copy)
        loss_slots[level, here] = value

    def finish_loss(level):
        here, size = lax.axis_index(AXES[level]), sizes[level]
        for step in range(1, size):
            source = lax.rem(here + size - step, size)
            remote(
                loss_send.at[level],
                loss_slots.at[level, source],
                loss_send_sem.at[level, step - 1],
                loss_recv_sem.at[level, step - 1],
                {AXES[level]: source},
            ).wait_recv()
        value = loss_slots[level, 0]
        for index in range(1, size):
            value = value + loss_slots[level, index]
        return value

    start_loss(0, loss)
    adj_smooth = adj_smooth + finish_carry(2, 1, False, False)
    d_filtered = jnp.where(ending, adj_smooth, product(split(adj_smooth), blend))
    adj_filter = local_scan(d_filtered, 0, False, True)
    start_carry(3, adj_filter, True)
    reduce_a.finish_scatter(0)
    reduce_a.start_scatter(1)
    start_loss(1, finish_loss(0))
    adj_filter = adj_filter + finish_carry(3, 0, False, True)

    d_observed = product(split(adj_filter), gain).astype(SHORT)
    reduce_a.finish_scatter(1)
    reduce_a.start_scatter(2)
    start_loss(2, finish_loss(1))
    back = [dot(d_observed, second_ref[tap], ((1,), (1,))) for tap in range(KERNEL_TAPS)]
    pieces = [jnp.zeros((SECOND_SPACING, channels), WIDE)] * (reach // SECOND_SPACING)
    for tap in range(KERNEL_TAPS):
        for part in range(frame_length // SECOND_SPACING):
            rows = back[tap][part * SECOND_SPACING : (part + 1) * SECOND_SPACING]
            pieces[tap + part] = pieces[tap + part] + rows
    d_preact = jnp.concatenate(pieces) * slope[...]
    padded = []
    for tap in range(KERNEL_TAPS):
        before = low + (tap - 1) * FIRST_SPACING
        after = ext.shape[0] - reach - before
        padded.append(
            jnp.concatenate(
                [
                    jnp.zeros((before, channels), WIDE),
                    d_preact,
                    jnp.zeros((after, channels), WIDE),
                ]
            )
        )
    wide = split(jnp.concatenate(padded, axis=1))
    signal = ext[...]
    grad_first = dot(signal, wide[0], ((0,), (0,))) + dot(signal, wide[1], ((0,), (0,)))
    grad_second = dot(spaced, d_observed, ((0,), (0,)))
    second_rows = KERNEL_TAPS * channels
    refs_b[0][0:second_rows] = grad_second
    for tap in range(KERNEL_TAPS):
        start = second_rows + tap * state
        refs_b[0][start : start + state] = grad_first[:, tap * channels : (tap + 1) * channels]
    used = second_rows + KERNEL_TAPS * state
    if refs_b[0].shape[0] > used:
        refs_b[0][used:] = jnp.zeros((refs_b[0].shape[0] - used, 128), WIDE)

    reduce_b.start_scatter(0)
    reduce_a.finish_scatter(2)
    reduce_a.start_gather(2)
    reduce_b.finish_scatter(0)
    reduce_b.start_scatter(1)
    reduce_a.finish_gather(2)
    reduce_a.start_gather(1)
    reduce_b.finish_scatter(1)
    reduce_b.start_scatter(2)
    reduce_a.finish_gather(1)
    reduce_a.start_gather(0)
    reduce_b.finish_scatter(2)
    reduce_b.start_gather(2)
    reduce_a.finish_gather(0)
    read_out[:, 0:128] = refs_a[1][0:state].astype(WIDE)
    read_out[:, 128:256] = refs_a[1][state:read_rows].astype(WIDE)
    loss_out[0] = jnp.sum(finish_loss(2))
    reduce_b.finish_gather(2)
    reduce_b.start_gather(1)
    reduce_b.finish_gather(1)
    reduce_b.start_gather(0)
    reduce_b.finish_gather(0)
    for tap in range(KERNEL_TAPS):
        second_out[tap] = refs_b[1][tap * channels : (tap + 1) * channels].astype(WIDE)
        start = second_rows + tap * state
        first_out[tap] = refs_b[1][start : start + state].astype(WIDE)

    @pl.when(jnp.logical_not(last_block))
    def _():
        to_next().wait_send()

    @pl.when(jnp.logical_not(first_block))
    def _():
        to_previous().wait_send()

    for index in range(4):
        drain_carry(index, index % 2 == 1)
    reduce_a.drain()
    reduce_b.drain()
    for copy in loss_pending:
        copy.wait_send()


def reduction_scratch(rows, sizes, kept):
    piece, left = [], rows
    for size in sizes:
        left //= size
        piece.append(left)
    before = [rows] + piece[:-1]
    most = max(sizes)
    return [
        pltpu.VMEM((rows, 128), WIDE),
        pltpu.VMEM((rows, 128), kept),
        *[pltpu.VMEM((count, 128), SHORT) for count in before],
        *[pltpu.VMEM((size - 1, count, 128), SHORT) for size, count in zip(sizes, piece)],
        *[pltpu.VMEM((count, 128), WIDE) for count in piece[:-1]],
        pltpu.SemaphoreType.DMA((6, most)),
        pltpu.SemaphoreType.DMA((6, most)),
    ]


def body(frames, *parameters):
    cores = lax.axis_size("state")
    blocks = lax.axis_size("tm") * cores
    sizes = tuple(lax.axis_size(axis) for axis in AXES)
    frame_length, state = frames.shape[1], frames.shape[2]
    channels = parameters[1].shape[2]
    levels = frame_length.bit_length() - 1 + (blocks - 1).bit_length()
    slots = max(8, 1 << (blocks - 1).bit_length())
    unit = 16 * math.prod(sizes)
    rows_a = -(-2 * state // unit) * unit
    rows_b = -(-(KERNEL_TAPS * (state + channels)) // unit) * unit
    most = max(sizes)
    dims = (blocks, cores, sizes, frames.shape[0] * sizes[1], frame_length * blocks, levels)
    vmem = pl.BlockSpec(memory_space=pltpu.VMEM)
    return tuple(
        pl.pallas_call(
            functools.partial(kernel, dims),
            out_shape=(
                jax.ShapeDtypeStruct((1, frame_length, state), WIDE),
                jax.ShapeDtypeStruct((KERNEL_TAPS, state, channels), WIDE),
                jax.ShapeDtypeStruct((KERNEL_TAPS, channels, channels), WIDE),
                jax.ShapeDtypeStruct((state, state), WIDE),
                jax.ShapeDtypeStruct((1,), WIDE),
            ),
            in_specs=[vmem] * 8,
            out_specs=(vmem, vmem, vmem, vmem, pl.BlockSpec(memory_space=pltpu.SMEM)),
            scratch_shapes=[
                pltpu.VMEM((frame_length + 2 * EDGE, state), SHORT),
                pltpu.VMEM((2, levels, state, state), SHORT),
                pltpu.VMEM((2, levels, state, state), SHORT),
                pltpu.VMEM((4, 1, state), WIDE),
                pltpu.VMEM((4, slots, 1, state), WIDE),
                pltpu.VMEM((frame_length + 2 * SECOND_SPACING, channels), WIDE),
                pltpu.SemaphoreType.DMA((2,)),
                pltpu.SemaphoreType.DMA((2,)),
                pltpu.SemaphoreType.DMA((4, blocks)),
                pltpu.SemaphoreType.DMA((4, blocks)),
                pltpu.VMEM((3, 1, 128), WIDE),
                pltpu.VMEM((3, most, 1, 128), WIDE),
                pltpu.SemaphoreType.DMA((3, most)),
                pltpu.SemaphoreType.DMA((3, most)),
                *reduction_scratch(rows_a, sizes, SHORT),
                *reduction_scratch(rows_b, sizes, WIDE),
            ],
            compiler_params=pltpu.CompilerParams(
                collective_id=0, has_side_effects=True, vmem_limit_bytes=48 * 1024 * 1024
            ),
        )(frames, *parameters)
    )


def solution(mesh):
    return jax.shard_map(
        body,
        mesh=mesh,
        in_specs=(P(("groups", "dp"), ("tm", "state"), None), P(), P(), P(), P(), P(), P(), P()),
        out_specs=(
            P(("groups", "dp"), ("tm", "state"), None),
            P("groups", None, None),
            P("groups", None, None),
            P("groups", None),
            P("groups"),
        ),
        check_vma=False,
    )
```

time: 313 us -> 83 us (0.27)
  matrix products: 88.9 us -> 0 us
  Pallas kernels: 0 us -> 70 us
  blocking collectives: 69.6 us -> 0 us
  waiting for transfers between devices: 64.1 us -> 0 us
  local copies, waits for them, and re-layouts: 46.8 us -> 10.1 us
  starting transfers between devices: 17.6 us -> 0 us
  between operations: 15.7 us -> 2.47 us
  other arithmetic: 5.64 us -> 0 us
    dot_general x128 -> x0, matrix products: 88.9 us -> none  [the longest x32 37.3 us: combine(): jnp.dot(earlier[1], later[0], precision=HIGHEST) + later[1]]
    pallas_call x0 -> x1, Pallas kernels: none -> 70 us  [body(): pl.pallas_call(functools.partial(kernel, dims), out_shape=(jax.ShapeDtype...]
    psum x1 -> x0, waiting for transfers between devices: 61.3 us -> none  [body(): lax.psum((first_layer_gradient, second_layer_gradient, grad_read, loss_pa...]
    all_gather x4 -> x0, blocking collectives: 41.2 us -> none  [prefix_2(): everything = jax.tree.map(lambda part: lax.all_gather(part, axis), array)]
    psum x1 -> x0, blocking collectives: 28.3 us -> none  [body(): lax.psum((first_layer_gradient, second_layer_gradient, grad_read, loss_pa...]
    concatenate x16 -> x0, local copies, waits for them, and re-layouts: 24.7 us -> none  [propagate(): carried_rows = jnp.concatenate([carried_rows, further])]
    ppermute x6 -> x0, starting transfers between devices: 17.4 us -> none  [the longest x3 11.6 us: padded_2(): before = lax.ppermute(last, axis, up)]
    unnamed x89 -> x20, local copies, waits for them, and re-layouts: 14.5 us -> 10.1 us
  transfers between devices with their start and end apart: 11 -> 0, of which waited for: 3 -> 0; matrix products, arithmetic and copies ran while one was open for 37% -> 0% of each run, Pallas kernels for 0% -> 0%
where the time goes in v1:
time: 83 us; the launch traced here: 82.6 us
  Pallas kernels  70 us (84%)
  local copies, waits for them, and re-layouts  10.1 us (12%)
  between operations  2.47 us (3%)
    pallas_call x1, Pallas kernels, body(): pl.pallas_call(functools.partial(kernel, dims), out_shape=(jax.ShapeDtype...  70 us
    unnamed x20, local copies, waits for them, and re-layouts  10.1 us

profile of v1, /device:TPU:1, one launch (start us, length us, event | category | flops | bytes accessed | tf_op | source)
XLA Modules:
  0.0 82.6 jit_solution(7642360165757409834)
XLA Ops:
  0.6 0.0 copy-start
  0.6 0.9 %copy-done = f32[256,256]{1,0:T(8,128)S(1)} copy-done((f32[256,256]{1,0:T(8,128)S(1)}, f32[256,256]{1,0:T(8,128)}, u32[]{:S(2)}) %copy-start) | copy-done | bytes 262168
  1.6 0.0 copy-start.1
  1.6 0.9 %copy-done.1 = f32[256,256]{1,0:T(8,128)S(1)} copy-done((f32[256,256]{1,0:T(8,128)S(1)}, f32[256,256]{1,0:T(8,128)}, u32[]{:S(2)}) %copy-start.1) | copy-done | bytes 262168
  2.5 0.0 copy-start.2
  2.5 0.9 %copy-done.2 = f32[256,256]{1,0:T(8,128)S(1)} copy-done((f32[256,256]{1,0:T(8,128)S(1)}, f32[256,256]{1,0:T(8,128)}, u32[]{:S(2)}) %copy-start.2) | copy-done | bytes 262168
  3.5 0.0 copy-start.3
  3.5 0.9 %copy-done.3 = f32[256,256]{1,0:T(8,128)S(1)} copy-done((f32[256,256]{1,0:T(8,128)S(1)}, f32[256,256]{1,0:T(8,128)}, u32[]{:S(2)}) %copy-start.3) | copy-done | bytes 262168
  4.4 0.0 copy-start.4
  4.4 0.9 %copy-done.4 = bf16[3,256,128]{2,1,0:T(8,128)(2,1)S(1)} copy-done((bf16[3,256,128]{2,1,0:T(8,128)(2,1)S(1)}, bf16[3,256,128]{2,1,0:T(8,128)(2,1)}, u32[]{:S(2)}) %copy-start.4) | copy-done | bytes 196632
  5.4 0.0 copy-start.5
  5.4 0.9 %copy-done.5 = f32[256,128]{1,0:T(8,128)S(1)} copy-done((f32[256,128]{1,0:T(8,128)S(1)}, f32[256,128]{1,0:T(8,128)}, u32[]{:S(2)}) %copy-start.5) | copy-done | bytes 131096
  6.3 0.0 copy-start.6
  6.3 0.9 %copy-done.6 = bf16[3,128,128]{2,1,0:T(8,128)(2,1)S(1)} copy-done((bf16[3,128,128]{2,1,0:T(8,128)(2,1)S(1)}, bf16[3,128,128]{2,1,0:T(8,128)(2,1)}, u32[]{:S(2)}) %copy-start.6) | copy-done | bytes 98328
  7.2 0.0 copy-start.7
  7.2 0.8 %copy-done.7 = bf16[1,128,256]{2,1,0:T(8,128)(2,1)S(1)} copy-done((bf16[1,128,256]{2,1,0:T(8,128)(2,1)S(1)}, bf16[1,128,256]{2,1,0:T(8,128)(2,1)}, u32[]{:S(2)}) %copy-start.7) | copy-done | bytes 65560
  8.0 70.0 %shard_map.119 = (f32[1,128,256]{2,1,0:T(8,128)S(1)}, f32[3,256,128]{2,1,0:T(8,128)S(1)}, f32[3,128,128]{2,1,0:T(8,128)S(1)}, f32[256,256]{1,0:T(8,128)S(1)}, f32[1]{0:T(128)}) custom-call(bf16[1,128,256]{2,1,0:T(8,128)(2,1)S(1)} %copy-done.7, bf16[3,256,128]{2,1,0:T(8,128)(2,1)S(1)} %copy-done.4, bf16[3,128,128]{2,1,0:T(8,128)(2,1)S(1)} %copy-done.6, ...), custom_call_target="tpu_custom_call" | custom-call | tf_op jit(solution)/shard_map/pallas_call | solution.py:518
  78.0 0.7 copy.18
  78.7 0.7 copy.19
  79.4 0.7 copy.20
  80.1 0.7 copy.21
Async XLA Ops:
  0.6 1.0 %copy-start = (f32[256,256]{1,0:T(8,128)S(1)}, f32[256,256]{1,0:T(8,128)}, u32[]{:S(2)}) copy-start(f32[256,256]{1,0:T(8,128)} %refs_3_.1) | copy-start | bytes 786436
  1.6 0.9 %copy-start.1 = (f32[256,256]{1,0:T(8,128)S(1)}, f32[256,256]{1,0:T(8,128)}, u32[]{:S(2)}) copy-start(f32[256,256]{1,0:T(8,128)} %refs_5_.1) | copy-start | bytes 786436
  2.5 0.9 %copy-start.2 = (f32[256,256]{1,0:T(8,128)S(1)}, f32[256,256]{1,0:T(8,128)}, u32[]{:S(2)}) copy-start(f32[256,256]{1,0:T(8,128)} %refs_6_.1) | copy-start | bytes 786436
  3.5 0.9 %copy-start.3 = (f32[256,256]{1,0:T(8,128)S(1)}, f32[256,256]{1,0:T(8,128)}, u32[]{:S(2)}) copy-start(f32[256,256]{1,0:T(8,128)} %refs_7_.1) | copy-start | bytes 786436
  4.4 0.9 %copy-start.4 = (bf16[3,256,128]{2,1,0:T(8,128)(2,1)S(1)}, bf16[3,256,128]{2,1,0:T(8,128)(2,1)}, u32[]{:S(2)}) copy-start(bf16[3,256,128]{2,1,0:T(8,128)(2,1)} %refs_1_.1) | copy-start | bytes 589828
  5.4 0.9 %copy-start.5 = (f32[256,128]{1,0:T(8,128)S(1)}, f32[256,128]{1,0:T(8,128)}, u32[]{:S(2)}) copy-start(f32[256,128]{1,0:T(8,128)} %refs_4_.1) | copy-start | bytes 393220
  6.3 0.9 %copy-start.6 = (bf16[3,128,128]{2,1,0:T(8,128)(2,1)S(1)}, bf16[3,128,128]{2,1,0:T(8,128)(2,1)}, u32[]{:S(2)}) copy-start(bf16[3,128,128]{2,1,0:T(8,128)(2,1)} %refs_2_.1) | copy-start | bytes 294916
  7.2 0.8 %copy-start.7 = (bf16[1,128,256]{2,1,0:T(8,128)(2,1)S(1)}, bf16[1,128,256]{2,1,0:T(8,128)(2,1)}, u32[]{:S(2)}) copy-start(bf16[1,128,256]{2,1,0:T(8,128)(2,1)} %refs_0_.1) | copy-start | bytes 196612

commit v2 on v1

--- a/solution.py
+++ b/solution.py
@@ -136,8 +136,9 @@
 
 def kernel(dims, *refs):
     blocks, cores, sizes, windows, frames_total, levels = dims
-    (frames_ref, first_ref, second_ref, readout_ref, gain_ref) = refs[:5]
-    (transition_ref, smoother_ref, blend_ref) = refs[5:8]
+    frames_ref, sources = refs[0], refs[1:8]
+    (first_ref, second_ref, readout_ref, gain_ref) = refs[51:55]
+    (transition_ref, smoother_ref, blend_ref, fetch_sem) = refs[55:59]
     (smoothed_out, first_out, second_out, read_out, loss_out) = refs[8:13]
     (ext, power_high, power_low, ends, arrivals, slope) = refs[13:19]
     (halo_send, halo_recv, carry_send, carry_recv) = refs[19:23]
@@ -152,9 +153,29 @@
     def device(at):
         return {"tm": at // cores, "state": lax.rem(at, cores)}
 
-    ext[...] = jnp.zeros_like(ext)
+    center = ext.at[EDGE : EDGE + frame_length]
+    fetches = [
+        pltpu.make_async_copy(src, dst, fetch_sem.at[index])
+        for index, (src, dst) in enumerate(
+            zip((*sources, frames_ref.at[0]), (*refs[51:58], center))
+        )
+    ]
+    fetch_first, fetch_second, fetch_readout, fetch_gain = fetches[:4]
+    fetch_transition, fetch_smoother, fetch_blend, fetch_frames = fetches[4:]
+    for fetch in (
+        fetch_transition,
+        fetch_frames,
+        fetch_first,
+        fetch_second,
+        fetch_gain,
+        fetch_smoother,
+        fetch_blend,
+        fetch_readout,
+    ):
+        fetch.start()
+    ext[0:EDGE] = jnp.zeros((EDGE, state), SHORT)
+    ext[EDGE + frame_length :] = jnp.zeros((EDGE, state), SHORT)
     arrivals[...] = jnp.zeros_like(arrivals)
-    ext[EDGE : EDGE + frame_length] = frames_ref[0]
     barrier = pltpu.get_barrier_semaphore()
     for step in range(1, blocks):
         pl.semaphore_signal(
@@ -201,14 +222,20 @@
     def power(which, level):
         return power_high[which, level], power_low[which, level]
 
-    for which, ref in enumerate((transition_ref, smoother_ref)):
-        held = ref[...]
-        for level in range(levels):
+    def store_powers(which, held, start, stop):
+        for level in range(start, stop):
             power_high[which, level], power_low[which, level] = split(held)
             if level + 1 < levels:
                 held = square(held)
-
-    gain, readout, blend = [split(ref[...]) for ref in (gain_ref, readout_ref, blend_ref)]
+        return held
+
+    fetch_transition.wait()
+    next_power = store_powers(0, transition_ref[...], 0, local_levels)
+    fetch_first.wait()
+    fetch_second.wait()
+    fetch_gain.wait()
+    fetch_frames.wait()
+    gain = split(gain_ref[...])
 
     @pl.when(jnp.logical_not(first_block))
     def _():
@@ -332,6 +359,12 @@
 
     filtered = local_scan(drive, 0, True, False)
     start_carry(0, filtered, False)
+    store_powers(0, next_power, local_levels, levels)
+    fetch_smoother.wait()
+    store_powers(1, smoother_ref[...], 0, levels)
+    fetch_blend.wait()
+    fetch_readout.wait()
+    blend, readout = split(blend_ref[...]), split(readout_ref[...])
     filtered = filtered + finish_carry(0, 0, True, False)
     blended = jnp.where(ending, filtered, product(split(filtered), blend, True))
     smoothed = local_scan(blended, 1, True, True)
@@ -340,7 +373,7 @@
     smoothed_out[0] = smoothed
 
     smoothed_pair = split(smoothed)
-    miss = product(smoothed_pair, readout, True) - frames_ref[0].astype(WIDE)
+    miss = product(smoothed_pair, readout, True) - center[...].astype(WIDE)
     scale = 1.0 / (windows * frames_total)
     miss_pair = split(miss * scale)
     adj_smooth = local_scan(product(miss_pair, readout), 1, False, False)
@@ -505,6 +538,7 @@
     blocks = lax.axis_size("tm") * cores
     sizes = tuple(lax.axis_size(axis) for axis in AXES)
     frame_length, state = frames.shape[1], frames.shape[2]
+    hbm = pl.BlockSpec(memory_space=pltpu.HBM)
     channels = parameters[1].shape[2]
     levels = frame_length.bit_length() - 1 + (blocks - 1).bit_length()
     slots = max(8, 1 << (blocks - 1).bit_length())
@@ -524,7 +558,7 @@
                 jax.ShapeDtypeStruct((state, state), WIDE),
                 jax.ShapeDtypeStruct((1,), WIDE),
             ),
-            in_specs=[vmem] * 8,
+            in_specs=[hbm] * 8,
             out_specs=(vmem, vmem, vmem, vmem, pl.BlockSpec(memory_space=pltpu.SMEM)),
             scratch_shapes=[
                 pltpu.VMEM((frame_length + 2 * EDGE, state), SHORT),
@@ -543,6 +577,8 @@
                 pltpu.SemaphoreType.DMA((3, most)),
                 *reduction_scratch(rows_a, sizes, SHORT),
                 *reduction_scratch(rows_b, sizes, WIDE),
+                *[pltpu.VMEM(array.shape, array.dtype) for array in parameters],
+                pltpu.SemaphoreType.DMA((8,)),
             ],
             compiler_params=pltpu.CompilerParams(
                 collective_id=0, has_side_effects=True, vmem_limit_bytes=48 * 1024 * 1024

time: 83 us -> 78.4 us (0.945)
  Pallas kernels: 70 us -> 65.4 us
    pallas_call x1, Pallas kernels: 70 us -> 65.4 us  [body(): pl.pallas_call(functools.partial(kernel, dims), out_shape=(jax.ShapeDtype...]
where the time goes in v2:
time: 78.4 us; the launch traced here: 78 us
  Pallas kernels  65.4 us (83%)
  local copies, waits for them, and re-layouts  10.1 us (13%)
  between operations  2.47 us (3%)
    pallas_call x1, Pallas kernels, body(): pl.pallas_call(functools.partial(kernel, dims), out_shape=(jax.ShapeDtype...  65.4 us
    unnamed x20, local copies, waits for them, and re-layouts  10.1 us

profile of v2, /device:TPU:1, one launch (start us, length us, event | category | flops | bytes accessed | tf_op | source)
XLA Modules:
  0.0 78.0 jit_solution(11716927123340985619)
XLA Ops:
  0.6 0.0 copy-start
  0.6 0.9 %copy-done = f32[256,256]{1,0:T(8,128)S(1)} copy-done((f32[256,256]{1,0:T(8,128)S(1)}, f32[256,256]{1,0:T(8,128)}, u32[]{:S(2)}) %copy-start) | copy-done | bytes 262168
  1.6 0.0 copy-start.1
  1.6 0.9 %copy-done.1 = f32[256,256]{1,0:T(8,128)S(1)} copy-done((f32[256,256]{1,0:T(8,128)S(1)}, f32[256,256]{1,0:T(8,128)}, u32[]{:S(2)}) %copy-start.1) | copy-done | bytes 262168
  2.5 0.0 copy-start.2
  2.5 0.9 %copy-done.2 = f32[256,256]{1,0:T(8,128)S(1)} copy-done((f32[256,256]{1,0:T(8,128)S(1)}, f32[256,256]{1,0:T(8,128)}, u32[]{:S(2)}) %copy-start.2) | copy-done | bytes 262168
  3.5 0.0 copy-start.3
  3.5 0.9 %copy-done.3 = f32[256,256]{1,0:T(8,128)S(1)} copy-done((f32[256,256]{1,0:T(8,128)S(1)}, f32[256,256]{1,0:T(8,128)}, u32[]{:S(2)}) %copy-start.3) | copy-done | bytes 262168
  4.4 0.0 copy-start.4
  4.4 0.9 %copy-done.4 = bf16[3,256,128]{2,1,0:T(8,128)(2,1)S(1)} copy-done((bf16[3,256,128]{2,1,0:T(8,128)(2,1)S(1)}, bf16[3,256,128]{2,1,0:T(8,128)(2,1)}, u32[]{:S(2)}) %copy-start.4) | copy-done | bytes 196632
  5.4 0.0 copy-start.5
  5.4 0.9 %copy-done.5 = f32[256,128]{1,0:T(8,128)S(1)} copy-done((f32[256,128]{1,0:T(8,128)S(1)}, f32[256,128]{1,0:T(8,128)}, u32[]{:S(2)}) %copy-start.5) | copy-done | bytes 131096
  6.3 0.0 copy-start.6
  6.3 0.9 %copy-done.6 = bf16[3,128,128]{2,1,0:T(8,128)(2,1)S(1)} copy-done((bf16[3,128,128]{2,1,0:T(8,128)(2,1)S(1)}, bf16[3,128,128]{2,1,0:T(8,128)(2,1)}, u32[]{:S(2)}) %copy-start.6) | copy-done | bytes 98328
  7.2 0.0 copy-start.7
  7.2 0.8 %copy-done.7 = bf16[1,128,256]{2,1,0:T(8,128)(2,1)S(1)} copy-done((bf16[1,128,256]{2,1,0:T(8,128)(2,1)S(1)}, bf16[1,128,256]{2,1,0:T(8,128)(2,1)}, u32[]{:S(2)}) %copy-start.7) | copy-done | bytes 65560
  8.0 65.4 %shard_map.119 = (f32[1,128,256]{2,1,0:T(8,128)S(1)}, f32[3,256,128]{2,1,0:T(8,128)S(1)}, f32[3,128,128]{2,1,0:T(8,128)S(1)}, f32[256,256]{1,0:T(8,128)S(1)}, f32[1]{0:T(128)}) custom-call(bf16[1,128,256]{2,1,0:T(8,128)(2,1)S(1)} %copy-done.7, bf16[3,256,128]{2,1,0:T(8,128)(2,1)S(1)} %copy-done.4, bf16[3,128,128]{2,1,0:T(8,128)(2,1)S(1)} %copy-done.6, ...), custom_call_target="tpu_custom_call" | custom-call | tf_op jit(solution)/shard_map/pallas_call | solution.py:552
  73.4 0.7 copy.18
  74.0 0.7 copy.19
  74.8 0.7 copy.20
  75.5 0.7 copy.21
Async XLA Ops:
  0.6 1.0 %copy-start = (f32[256,256]{1,0:T(8,128)S(1)}, f32[256,256]{1,0:T(8,128)}, u32[]{:S(2)}) copy-start(f32[256,256]{1,0:T(8,128)} %refs_3_.1) | copy-start | bytes 786436
  1.6 0.9 %copy-start.1 = (f32[256,256]{1,0:T(8,128)S(1)}, f32[256,256]{1,0:T(8,128)}, u32[]{:S(2)}) copy-start(f32[256,256]{1,0:T(8,128)} %refs_5_.1) | copy-start | bytes 786436
  2.5 0.9 %copy-start.2 = (f32[256,256]{1,0:T(8,128)S(1)}, f32[256,256]{1,0:T(8,128)}, u32[]{:S(2)}) copy-start(f32[256,256]{1,0:T(8,128)} %refs_6_.1) | copy-start | bytes 786436
  3.5 0.9 %copy-start.3 = (f32[256,256]{1,0:T(8,128)S(1)}, f32[256,256]{1,0:T(8,128)}, u32[]{:S(2)}) copy-start(f32[256,256]{1,0:T(8,128)} %refs_7_.1) | copy-start | bytes 786436
  4.4 0.9 %copy-start.4 = (bf16[3,256,128]{2,1,0:T(8,128)(2,1)S(1)}, bf16[3,256,128]{2,1,0:T(8,128)(2,1)}, u32[]{:S(2)}) copy-start(bf16[3,256,128]{2,1,0:T(8,128)(2,1)} %refs_1_.1) | copy-start | bytes 589828
  5.4 0.9 %copy-start.5 = (f32[256,128]{1,0:T(8,128)S(1)}, f32[256,128]{1,0:T(8,128)}, u32[]{:S(2)}) copy-start(f32[256,128]{1,0:T(8,128)} %refs_4_.1) | copy-start | bytes 393220
  6.3 0.9 %copy-start.6 = (bf16[3,128,128]{2,1,0:T(8,128)(2,1)S(1)}, bf16[3,128,128]{2,1,0:T(8,128)(2,1)}, u32[]{:S(2)}) copy-start(bf16[3,128,128]{2,1,0:T(8,128)(2,1)} %refs_2_.1) | copy-start | bytes 294916
  7.2 0.8 %copy-start.7 = (bf16[1,128,256]{2,1,0:T(8,128)(2,1)S(1)}, bf16[1,128,256]{2,1,0:T(8,128)(2,1)}, u32[]{:S(2)}) copy-start(bf16[1,128,256]{2,1,0:T(8,128)(2,1)} %refs_0_.1) | copy-start | bytes 196612

commit v3 on v2

--- a/solution.py
+++ b/solution.py
@@ -430,6 +430,8 @@
     d_filtered = jnp.where(ending, adj_smooth, product(split(adj_smooth), blend))
     adj_filter = local_scan(d_filtered, 0, False, True)
     start_carry(3, adj_filter, True)
+    signal = ext[...].astype(WIDE).T.astype(SHORT)
+    spaced = spaced.astype(WIDE).T.astype(SHORT)
     reduce_a.finish_scatter(0)
     reduce_a.start_scatter(1)
     start_loss(1, finish_loss(0))
@@ -460,9 +462,8 @@
             )
         )
     wide = split(jnp.concatenate(padded, axis=1))
-    signal = ext[...]
-    grad_first = dot(signal, wide[0], ((0,), (0,))) + dot(signal, wide[1], ((0,), (0,)))
-    grad_second = dot(spaced, d_observed, ((0,), (0,)))
+    grad_first = dot(signal, wide[0], ((1,), (0,))) + dot(signal, wide[1], ((1,), (0,)))
+    grad_second = dot(spaced, d_observed, ((1,), (0,)))
     second_rows = KERNEL_TAPS * channels
     refs_b[0][0:second_rows] = grad_second
     for tap in range(KERNEL_TAPS):

time: 78.4 us -> 78.4 us (level)
  no operation moved by 1% of the time
where the time goes in v3:
time: 78.4 us; the launch traced here: 78 us
  Pallas kernels  65.4 us (83%)
  local copies, waits for them, and re-layouts  10.1 us (13%)
  between operations  2.47 us (3%)
    pallas_call x1, Pallas kernels, body(): pl.pallas_call(functools.partial(kernel, dims), out_shape=(jax.ShapeDtype...  65.4 us
    unnamed x20, local copies, waits for them, and re-layouts  10.1 us

profile of v3, /device:TPU:1, one launch (start us, length us, event | category | flops | bytes accessed | tf_op | source)
XLA Modules:
  0.0 78.0 jit_solution(14879489069287381077)
XLA Ops:
  0.6 0.0 copy-start
  0.6 0.9 %copy-done = f32[256,256]{1,0:T(8,128)S(1)} copy-done((f32[256,256]{1,0:T(8,128)S(1)}, f32[256,256]{1,0:T(8,128)}, u32[]{:S(2)}) %copy-start) | copy-done | bytes 262168
  1.6 0.0 copy-start.1
  1.6 0.9 %copy-done.1 = f32[256,256]{1,0:T(8,128)S(1)} copy-done((f32[256,256]{1,0:T(8,128)S(1)}, f32[256,256]{1,0:T(8,128)}, u32[]{:S(2)}) %copy-start.1) | copy-done | bytes 262168
  2.5 0.0 copy-start.2
  2.5 0.9 %copy-done.2 = f32[256,256]{1,0:T(8,128)S(1)} copy-done((f32[256,256]{1,0:T(8,128)S(1)}, f32[256,256]{1,0:T(8,128)}, u32[]{:S(2)}) %copy-start.2) | copy-done | bytes 262168
  3.5 0.0 copy-start.3
  3.5 0.9 %copy-done.3 = f32[256,256]{1,0:T(8,128)S(1)} copy-done((f32[256,256]{1,0:T(8,128)S(1)}, f32[256,256]{1,0:T(8,128)}, u32[]{:S(2)}) %copy-start.3) | copy-done | bytes 262168
  4.4 0.0 copy-start.4
  4.4 0.9 %copy-done.4 = bf16[3,256,128]{2,1,0:T(8,128)(2,1)S(1)} copy-done((bf16[3,256,128]{2,1,0:T(8,128)(2,1)S(1)}, bf16[3,256,128]{2,1,0:T(8,128)(2,1)}, u32[]{:S(2)}) %copy-start.4) | copy-done | bytes 196632
  5.4 0.0 copy-start.5
  5.4 0.9 %copy-done.5 = f32[256,128]{1,0:T(8,128)S(1)} copy-done((f32[256,128]{1,0:T(8,128)S(1)}, f32[256,128]{1,0:T(8,128)}, u32[]{:S(2)}) %copy-start.5) | copy-done | bytes 131096
  6.3 0.0 copy-start.6
  6.3 0.9 %copy-done.6 = bf16[3,128,128]{2,1,0:T(8,128)(2,1)S(1)} copy-done((bf16[3,128,128]{2,1,0:T(8,128)(2,1)S(1)}, bf16[3,128,128]{2,1,0:T(8,128)(2,1)}, u32[]{:S(2)}) %copy-start.6) | copy-done | bytes 98328
  7.2 0.0 copy-start.7
  7.2 0.8 %copy-done.7 = bf16[1,128,256]{2,1,0:T(8,128)(2,1)S(1)} copy-done((bf16[1,128,256]{2,1,0:T(8,128)(2,1)S(1)}, bf16[1,128,256]{2,1,0:T(8,128)(2,1)}, u32[]{:S(2)}) %copy-start.7) | copy-done | bytes 65560
  8.0 65.4 %shard_map.119 = (f32[1,128,256]{2,1,0:T(8,128)S(1)}, f32[3,256,128]{2,1,0:T(8,128)S(1)}, f32[3,128,128]{2,1,0:T(8,128)S(1)}, f32[256,256]{1,0:T(8,128)S(1)}, f32[1]{0:T(128)}) custom-call(bf16[1,128,256]{2,1,0:T(8,128)(2,1)S(1)} %copy-done.7, bf16[3,256,128]{2,1,0:T(8,128)(2,1)S(1)} %copy-done.4, bf16[3,128,128]{2,1,0:T(8,128)(2,1)S(1)} %copy-done.6, ...), custom_call_target="tpu_custom_call" | custom-call | tf_op jit(solution)/shard_map/pallas_call | solution.py:553
  73.4 0.7 copy.18
  74.0 0.7 copy.19
  74.8 0.7 copy.20
  75.5 0.7 copy.21
Async XLA Ops:
  0.6 1.0 %copy-start = (f32[256,256]{1,0:T(8,128)S(1)}, f32[256,256]{1,0:T(8,128)}, u32[]{:S(2)}) copy-start(f32[256,256]{1,0:T(8,128)} %refs_3_.1) | copy-start | bytes 786436
  1.6 0.9 %copy-start.1 = (f32[256,256]{1,0:T(8,128)S(1)}, f32[256,256]{1,0:T(8,128)}, u32[]{:S(2)}) copy-start(f32[256,256]{1,0:T(8,128)} %refs_5_.1) | copy-start | bytes 786436
  2.5 0.9 %copy-start.2 = (f32[256,256]{1,0:T(8,128)S(1)}, f32[256,256]{1,0:T(8,128)}, u32[]{:S(2)}) copy-start(f32[256,256]{1,0:T(8,128)} %refs_6_.1) | copy-start | bytes 786436
  3.5 0.9 %copy-start.3 = (f32[256,256]{1,0:T(8,128)S(1)}, f32[256,256]{1,0:T(8,128)}, u32[]{:S(2)}) copy-start(f32[256,256]{1,0:T(8,128)} %refs_7_.1) | copy-start | bytes 786436
  4.4 0.9 %copy-start.4 = (bf16[3,256,128]{2,1,0:T(8,128)(2,1)S(1)}, bf16[3,256,128]{2,1,0:T(8,128)(2,1)}, u32[]{:S(2)}) copy-start(bf16[3,256,128]{2,1,0:T(8,128)(2,1)} %refs_1_.1) | copy-start | bytes 589828
  5.4 0.9 %copy-start.5 = (f32[256,128]{1,0:T(8,128)S(1)}, f32[256,128]{1,0:T(8,128)}, u32[]{:S(2)}) copy-start(f32[256,128]{1,0:T(8,128)} %refs_4_.1) | copy-start | bytes 393220
  6.3 0.9 %copy-start.6 = (bf16[3,128,128]{2,1,0:T(8,128)(2,1)S(1)}, bf16[3,128,128]{2,1,0:T(8,128)(2,1)}, u32[]{:S(2)}) copy-start(bf16[3,128,128]{2,1,0:T(8,128)(2,1)} %refs_2_.1) | copy-start | bytes 294916
  7.2 0.8 %copy-start.7 = (bf16[1,128,256]{2,1,0:T(8,128)(2,1)S(1)}, bf16[1,128,256]{2,1,0:T(8,128)(2,1)}, u32[]{:S(2)}) copy-start(bf16[1,128,256]{2,1,0:T(8,128)(2,1)} %refs_0_.1) | copy-start | bytes 196612
